TPU v7x, 32 devices: a whole 2x2x4 slice. The times are simulated.
32 devices in a mesh: grp: 1, ep: 16 (over z, y, x), sub: 2 (over core).
Axes of the slice: x: 2, y: 2, z: 4, core: 2. Of those that a mesh axis runs over, the one named last changes fastest.
Arguments:
- resid_in: bfloat16 [2048, 2048], P(('grp', 'ep', 'sub')), may hold values from -6 to 6
- query_input: bfloat16 [2048, 1024], P(('grp', 'ep', 'sub')), may hold values from -6 to 6
- key_input: bfloat16 [2048, 1024], P(('grp', 'ep', 'sub')), may hold values from -6 to 6
- value_input: bfloat16 [2048, 2048], P(('grp', 'ep', 'sub')), may hold values from -6 to 6
- gate_input: bfloat16 [2048, 2048], P(('grp', 'ep', 'sub')), may hold values from -6 to 6
- decay_log: float32 [16, 2048], P(None, ('grp', 'ep', 'sub')), may hold values from -1 to 0
- write_rate: float32 [16, 2048], P(None, ('grp', 'ep', 'sub')), may hold values from 0.05 to 0.95
- segments: int32 [32, 64], P(('grp', 'ep', 'sub')), may hold values from 0 to 3, never falling along the last dimension, each value on 1 to 32 neighbouring positions
- head_gain: float32 [128], replicated, may hold values from 0.1 to 1.9
- out_proj: bfloat16 [2048, 2048], P('sub'), may hold values from -0.125 to 0.125
- post_gain: float32 [2048], replicated, may hold values from 0.1 to 1.9
- block_exps: int32 [2048, 16], P(('grp', 'ep', 'sub')), may hold values from -9 to -5
- route_ids: int32 [2048, 10], P(('grp', 'ep', 'sub')), may hold values from 0 to 31, all different within a row; in each aligned block of 64 rows (0 to 63, 64 to 127, ...) at most 32 rows name the same one
- route_weights: float32 [2048, 10], P(('grp', 'ep', 'sub')), may hold values from 0.1 to 1
- w_gate_up: bfloat16 [32, 2048, 1024], P(('ep', 'sub')), may hold values from -0.125 to 0.125
- w_down: bfloat16 [32, 512, 2048], P(('ep', 'sub')), may hold values from -0.25 to 0.25
Outputs:
- layer_out: bfloat16 [2048, 2048], P(('grp', 'ep', 'sub'))
Inputs may be any that keep to these rules, and one draw needn't show every extreme that they name: `route_ids`: on the rows of one device no expert is named more than 32 times, a bound that some block reaches. `segments`: each device's row numbers its own sequences from 0 and never falls; a sequence has at most 32 tokens, and some has exactly that many.
All inputs are finite; a program needn't handle non-finite values.
Results may differ from a plain program's by a relative error of at most 0.014.
Values may be sent and summed in bfloat16 or wider, within the bound.
A program may use at most 128 MiB of HBM per device.

v0:
```python
import jax
import jax.numpy as jnp
from jax import lax
from jax.sharding import PartitionSpec as P

KH = 8
HALF_VALUE_HEADS = 16
DK = 128
DV = 128
TOPK = 10


def unit_rows(values_in):
    return values_in * lax.rsqrt(jnp.sum(values_in * values_in, -1, keepdims=True) + 1e-06)


def delta_rule(query_heads, key_heads, value_heads, log_decay, rate_rows, labels_all):
    head_count, length, key_width = key_heads.shape
    value_width = value_heads.shape[2]
    block_len = min(64, length)
    lower_mask = jnp.tril(jnp.ones((block_len, block_len), bool))
    strict_mask = jnp.tril(jnp.ones((block_len, block_len), jnp.float32), -1)
    identity = jnp.eye(block_len, dtype=jnp.float32)
    highest = lax.Precision.HIGHEST
    memory = jnp.zeros((head_count, key_width, value_width), jnp.float32)
    cumulative = jnp.cumsum(log_decay, axis=1)
    matched = labels_all[:, None] == labels_all[None, :]
    carried = jnp.zeros((block_len,), jnp.float32)
    spread = jnp.where(lower_mask, cumulative[:, :, None] - cumulative[:, None, :], 0.0)
    decayed = jnp.exp(spread) * (lower_mask & matched).astype(jnp.float32)
    key_inner = jnp.einsum("hid,hjd->hij", key_heads, key_heads, precision=highest)
    mixing = decayed * strict_mask * rate_rows[:, None, :] * key_inner
    entry_decay = jnp.exp(cumulative) * carried[None, :]
    target = value_heads - entry_decay[:, :, None] * jnp.einsum(
        "hid,hde->hie", key_heads, memory, precision=highest
    )
    update = lax.linalg.triangular_solve(identity + mixing, target, left_side=True, lower=True)
    scores = (
        decayed
        * rate_rows[:, None, :]
        * jnp.einsum("hid,hjd->hij", query_heads, key_heads, precision=highest)
    )
    output = entry_decay[:, :, None] * jnp.einsum(
        "hid,hde->hie", query_heads, memory, precision=highest
    )
    output = output + jnp.einsum("hij,hje->hie", scores, update, precision=highest)
    return output


def restore(quantized, exponents):
    shape = quantized.shape
    block_count = exponents.shape[-1]
    scaled = quantized.astype(jnp.float32).reshape(
        shape[:-1] + (block_count, shape[-1] // block_count)
    )
    scaled = scaled * jnp.exp2(exponents.astype(jnp.float32))[..., None]
    return scaled.astype(jnp.bfloat16).reshape(shape)


def expert_rows(rows_in, weights_in, gate_up, down):
    shape = rows_in.shape
    flat_rows = rows_in.reshape(-1, shape[-1])
    inner = jnp.dot(flat_rows, gate_up, preferred_element_type=jnp.float32)
    half_width = gate_up.shape[1] // 2
    expert_hidden = (jax.nn.silu(inner[:, :half_width]) * inner[:, half_width:]).astype(
        jnp.bfloat16
    )
    projected = jnp.dot(expert_hidden, down, preferred_element_type=jnp.float32)
    return (weights_in.reshape(-1)[:, None] * projected).astype(jnp.bfloat16).reshape(shape)


def per_device(
    resid_in,
    query_input,
    key_input,
    value_input,
    gate_input,
    decay_log,
    write_rate,
    segments,
    head_gain,
    out_proj,
    post_gain,
    block_exps,
    route_ids,
    route_weights,
    w_gate_up,
    w_down,
):
    tokens = resid_in.shape[0]
    model_width = resid_in.shape[1]
    repeat = HALF_VALUE_HEADS // KH
    query_heads = jnp.repeat(
        unit_rows(query_input.astype(jnp.float32).reshape(tokens, KH, DK)), repeat, axis=1
    ).transpose(1, 0, 2)
    key_heads = jnp.repeat(
        unit_rows(key_input.astype(jnp.float32).reshape(tokens, KH, DK)), repeat, axis=1
    ).transpose(1, 0, 2)
    value_heads = (
        value_input.astype(jnp.float32).reshape(tokens, HALF_VALUE_HEADS, DV).transpose(1, 0, 2)
    )
    mixer_out = delta_rule(
        query_heads, key_heads, value_heads, decay_log, write_rate, segments[0]
    ).transpose(1, 0, 2)
    head_normed = (
        mixer_out
        * lax.rsqrt(jnp.mean(mixer_out * mixer_out, -1, keepdims=True) + 1e-06)
        * head_gain
    )
    head_normed = head_normed * jax.nn.silu(
        gate_input.astype(jnp.float32).reshape(tokens, HALF_VALUE_HEADS, DV)
    )
    gated_out = head_normed.astype(jnp.bfloat16).reshape(tokens, HALF_VALUE_HEADS * DV)
    attended = jnp.dot(
        gated_out,
        lax.all_gather(out_proj, "sub", axis=0, tiled=True),
        preferred_element_type=jnp.float32,
    )
    hidden = (resid_in.astype(jnp.float32) + attended).astype(jnp.bfloat16)
    hidden_wide = hidden.astype(jnp.float32)
    normalized = (
        hidden_wide
        * lax.rsqrt(jnp.mean(hidden_wide * hidden_wide, -1, keepdims=True) + 1e-06)
        * post_gain
    )
    block_count = block_exps.shape[1]
    powers = jnp.exp2(block_exps.astype(jnp.float32))[:, :, None]
    quantized = jnp.clip(
        normalized.reshape(tokens, block_count, model_width // block_count) / powers, -448.0, 448.0
    )
    quantized = quantized.astype(jnp.bfloat16).reshape(tokens, model_width)
    devices = lax.axis_size(("ep", "sub"))
    capacity = min(tokens, 8 * tokens * TOPK // (5 * devices))
    flat_ids = route_ids.reshape(-1)
    pair_count = flat_ids.shape[0]
    matches = (flat_ids[:, None] == jnp.arange(devices, dtype=jnp.int32)[None, :]).astype(jnp.int32)
    ranking = jnp.sum(jnp.cumsum(matches, axis=0) * matches, axis=1) - 1
    slot_index = flat_ids * capacity + ranking
    sources = jnp.full((devices * capacity,), pair_count, jnp.int32)
    sources = (
        sources.at[slot_index]
        .set(jnp.arange(pair_count, dtype=jnp.int32))
        .reshape(devices, capacity)
    )
    token_slot = sources // TOPK
    quant_padded = jnp.concatenate([quantized, jnp.zeros((1, model_width), jnp.bfloat16)], axis=0)
    exps_padded = jnp.concatenate([block_exps, jnp.zeros((1, block_count), jnp.int32)], axis=0)
    weight_padded = jnp.concatenate(
        [route_weights.reshape(-1), jnp.zeros((1,), jnp.float32)], axis=0
    )
    send_quant = quant_padded[token_slot]
    send_exps = exps_padded[token_slot]
    send_weights = weight_padded[sources]
    answer = expert_rows(
        restore(
            lax.all_to_all(send_quant, ("ep", "sub"), split_axis=0, concat_axis=0, tiled=True),
            lax.all_to_all(send_exps, ("ep", "sub"), split_axis=0, concat_axis=0, tiled=True),
        ),
        lax.all_to_all(
            send_weights.astype(jnp.bfloat16),
            ("ep", "sub"),
            split_axis=0,
            concat_axis=0,
            tiled=True,
        ).astype(send_weights.dtype),
        w_gate_up[0],
        w_down[0],
    )
    returned = lax.all_to_all(answer, ("ep", "sub"), split_axis=0, concat_axis=0, tiled=True)
    gathered = returned.reshape(devices * capacity, model_width)[slot_index]
    summed = jnp.sum(gathered.astype(jnp.float32).reshape(tokens, TOPK, model_width), axis=1)
    return (hidden_wide + summed).astype(jnp.bfloat16)


def solution(mesh):
    return jax.shard_map(
        per_device,
        mesh=mesh,
        in_specs=(
            P(("grp", "ep", "sub"), None),
            P(("grp", "ep", "sub"), None),
            P(("grp", "ep", "sub"), None),
            P(("grp", "ep", "sub"), None),
            P(("grp", "ep", "sub"), None),
            P(None, ("grp", "ep", "sub")),
            P(None, ("grp", "ep", "sub")),
            P(("grp", "ep", "sub"), None),
            P(),
            P("sub", None),
            P(),
            P(("grp", "ep", "sub"), None),
            P(("grp", "ep", "sub"), None),
            P(("grp", "ep", "sub"), None),
            P(("ep", "sub"), None, None),
            P(("ep", "sub"), None, None),
        ),
        out_specs=P(("grp", "ep", "sub"), None),
        check_vma=False,
    )
```

profile of v0, /device:TPU:0, one launch (start us, length us, event | category | flops | bytes accessed | tf_op | source)
XLA Modules:
  0.0 382.5 jit_solution(1367202133912574056)
XLA Ops:
  8.3 1.5 reduce-window.6
  10.8 4.1 %scatter_custom_fusion = s32[1024]{0:T(1024)S(1)} fusion(s32[640]{0:T(1024)S(1)} %fusion.34, s32[640]{0:T(1024)S(1)} %iota.81, s32[]{:T(128)} %constant.27.clone.1), kind=kCustom, calls=%fused_computation.92 | custom fusion | bytes 4100 | tf_op jit(solution)/shard_map/scatter | solution.py:142
  15.1 6.8 %gather_fusion = bf16[1024]{0:T(1024)(128)(2,1)S(1)} fusion(bf16[641]{0:T(1024)(128)(2,1)S(1)} %pad_maximum_fusion, s32[1024]{0:T(1024)S(1)} %broadcast_clamp_fusion.1), kind=kCustom, calls=%fused_computation | custom fusion | bytes 8192 | tf_op jit(solution)/shard_map/gather | solution.py:153
  22.6 7.3 %all-to-all-start = ((bf16[32,1,32]{2,1,0:T(2,128)(2,1)}), bf16[32,1,32]{2,1,0:T(2,128)(2,1)S(1)}, u32[]{:S(2)}, u32[]{:S(2)}) async-start(bf16[32,1,32]{2,1,0:T(2,128)(2,1)} %convert_element_type.119), calls=%async_computation | async-start | bytes 32768 | tf_op jit(solution)/shard_map/all_to_all | solution.py:159
  30.3 0.8 copy.51
  32.0 1.0 fusion.9
  33.0 79.3 %custom-call.3 = f32[16,1,64,64]{2,3,1,0:T(8,128)} custom-call(f32[16,1,64,64]{3,2,1,0:T(8,128)S(1)} %fusion.9), custom_call_target="InvertDiagBlocksLowerTriangular" | custom-call | tf_op jit(solution)/shard_map/triangular_solve | solution.py:37
  112.4 2.8 gather_fusion.2
  115.4 0.8 reshape.395
  116.3 1.6 fusion.6
  117.9 2.0 fusion.21
  120.0 1.0 broadcast_in_dim.26
  121.0 1.0 convolution_multiply_fusion.2
  122.6 0.7 multiply_reduce_fusion.1
  123.4 5.2 %multiply_reduce_fusion = (f32[64]{0:T(128)S(1)}, f32[64,2048]{1,0:T(8,128)S(1)}) fusion(bf16[2048,2048]{1,0:T(8,128)(2,1)} %all-gather.2.cloned.1.call-done, bf16[64,2048]{1,0:T(8,128)(2,1)} %param.16, f32[128]{0:T(128)S(1)} %copy-done.11, f32[64,16,128]{2,0,1:T(8,128)S(1)} %get-tuple-element.10, f32[64,16]{0,1:T(8,128)S(1)} %add_rsqrt_fusion.2, ...), kind=kOutput, calls=%fused_computation.43 | convolution fusion | flops 538836928 | bytes 9966336 | tf_op jit(solution)/shard_map/dot_general | solution.py:114
  128.6 5.8 %all-to-all-start.2 = ((s32[32,1,512]{2,1,0:T(1,128)}), s32[32,1,512]{2,1,0:T(1,128)S(1)}, u32[]{:S(2)}, u32[]{:S(2)}) async-start(s32[32,1,512]{2,1,0:T(1,128)} %reshape.395), calls=%async_computation.2 | async-start | bytes 131072 | tf_op jit(solution)/shard_map/all_to_all | solution.py:157
  134.9 6.0 %gather_fusion.1 = bf16[1024,2048]{1,0:T(8,128)(2,1)} fusion(bf16[65,2048]{1,0:T(8,128)(2,1)S(1)} %concatenate.10, s32[1024]{0:T(1024)S(1)} %broadcast_clamp_fusion), kind=kCustom, calls=%fused_computation.1 | custom fusion | bytes 8392704 | tf_op jit(solution)/shard_map/gather | solution.py:151
  141.0 0.9 all-to-all-done.2
  141.8 5.1 %all-to-all-start.1 = ((bf16[32,32,2048]{2,1,0:T(8,128)(2,1)}), bf16[32,32,2048]{2,1,0:T(8,128)(2,1)}, u32[]{:S(2)}, u32[]{:S(2)}) async-start(bf16[32,32,2048]{2,1,0:T(8,128)(2,1)} %bitcast.128), calls=%async_computation.1 | async-start | bytes 8388608 | tf_op jit(solution)/shard_map/all_to_all | solution.py:156
  147.6 0.8 reduce.8
  148.8 4.6 %mul.215 = f32[32,32,16,128]{3,2,1,0:T(8,128)} broadcast(f32[32,32,16]{2,1,0:T(8,128)S(1)} %copy.67), dimensions={0,1,2} | broadcast | bytes 8454144 | tf_op jit(solution)/shard_map/mul | solution.py:56
  153.3 9.3 %mul.216 = f32[32,32,2048]{2,1,0:T(8,128)} reshape(f32[32,32,16,128]{3,2,1,0:T(8,128)} %mul.215) | data formatting | bytes 16777216 | tf_op jit(solution)/shard_map/mul | solution.py:56
  162.6 78.2 %all-to-all-done.1 = bf16[32,32,2048]{2,1,0:T(8,128)(2,1)} async-done(((bf16[32,32,2048]{2,1,0:T(8,128)(2,1)}), bf16[32,32,2048]{2,1,0:T(8,128)(2,1)}, u32[]{:S(2)}, u32[]{:S(2)}) %all-to-all-start.1) | async-done | bytes 4194336 | tf_op jit(solution)/shard_map/all_to_all | solution.py:156
  240.8 6.2 %multiply_convert_fusion.1 = bf16[32,32,2048]{2,1,0:T(8,128)(2,1)S(1)} fusion(f32[32,32,2048]{2,1,0:T(8,128)} %mul.216, bf16[32,32,2048]{2,1,0:T(8,128)(2,1)} %all-to-all-done.1), kind=kLoop, calls=%fused_computation.6 | loop fusion | flops 6291456 | bytes 16777216 | tf_op jit(solution)/shard_map/convert_element_type | solution.py:57
  247.0 4.5 %fusion = f32[1024,1024]{1,0:T(8,128)S(1)} fusion(bf16[1024,2048]{1,0:T(8,128)(2,1)S(1)} %bitcast.135, bf16[1,2048,1024]{2,1,0:T(8,128)(2,1)S(1)} %copy-done.13), kind=kOutput, calls=%fused_computation.7 | convolution fusion | flops 4294967296 | bytes 12582912 | tf_op jit(solution)/shard_map/dot_general | solution.py:63
  251.5 4.4 %multiply_convert_fusion = bf16[1024,2048]{1,0:T(8,128)(2,1)} fusion(f32[1024]{0:T(1024)S(1)} %reshape.333, bf16[1,512,2048]{2,1,0:T(8,128)(2,1)S(1)} %copy-done, f32[1024,1024]{1,0:T(8,128)S(1)} %fusion), kind=kOutput, calls=%fused_computation.5 | convolution fusion | flops 2154823680 | bytes 10489856 | tf_op jit(solution)/shard_map/dot_general | solution.py:68
  256.0 4.3 %all-to-all-start.3 = ((bf16[32,32,2048]{2,1,0:T(8,128)(2,1)}), bf16[32,32,2048]{2,1,0:T(8,128)(2,1)}, u32[]{:S(2)}, u32[]{:S(2)}) async-start(bf16[32,32,2048]{2,1,0:T(8,128)(2,1)} %bitcast.134), calls=%async_computation.3 | async-start | bytes 8388608 | tf_op jit(solution)/shard_map/all_to_all | solution.py:169
  260.3 93.8 %all-to-all-done.3 = bf16[32,32,2048]{2,1,0:T(8,128)(2,1)} async-done(((bf16[32,32,2048]{2,1,0:T(8,128)(2,1)}), bf16[32,32,2048]{2,1,0:T(8,128)(2,1)}, u32[]{:S(2)}, u32[]{:S(2)}) %all-to-all-start.3) | async-done | bytes 4194336 | tf_op jit(solution)/shard_map/all_to_all | solution.py:169
  354.1 9.7 %gather_fusion.3 = bf16[640,2048]{1,0:T(8,128)(2,1)} fusion(bf16[1024,2048]{1,0:T(8,128)(2,1)} %bitcast.20, s32[1024]{0:T(1024)S(1)} %pad_clamp_fusion), kind=kCustom, calls=%fused_computation.3 | custom fusion | bytes 5245440 | tf_op jit(solution)/shard_map/gather | solution.py:170
  363.8 5.8 %reshape.334 = f32[64,10,2048]{2,1,0:T(8,128)} reshape(bf16[640,2048]{1,0:T(8,128)(2,1)} %gather_fusion.3) | data formatting | bytes 7864320 | tf_op jit(solution)/shard_map/convert_element_type | solution.py:171
  369.6 5.3 %reduce_sum.59 = f32[64,2048]{1,0:T(8,128)S(1)} reduce(f32[64,10,2048]{2,1,0:T(8,128)} %reshape.334, f32[]{:T(128)} %constant.21.clone.1), dimensions={1}, to_apply=%region_9.10 | reduce | flops 1179648 | bytes 5767172 | tf_op jit(solution)/shard_map/reduce_sum | solution.py:171
  374.9 0.8 add_convert_fusion
  (91 shorter events, 7.4 us)
Async XLA Ops:
  6.5 245.0 %copy-start = (bf16[1,512,2048]{2,1,0:T(8,128)(2,1)S(1)}, bf16[1,512,2048]{2,1,0:T(8,128)(2,1)}, u32[]{:S(2)}) copy-start(bf16[1,512,2048]{2,1,0:T(8,128)(2,1)} %param.31) | copy-start | bytes 6291460
  6.5 0.8 copy-start.3
  6.5 1.2 copy-start.9
  6.5 116.8 %all-gather.2.cloned.1.call-start = ((), (), s32[]{:S(2)}) async-start(), calls=%async_computation.4 | async-start | bytes 12582912 | tf_op jit(solution)/shard_map/all_gather | solution.py:116
  10.2 0.6 copy-start.6
  15.0 14.9 %copy-start.1 = (bf16[64,1024]{1,0:T(8,128)(2,1)S(1)}, bf16[64,1024]{1,0:T(8,128)(2,1)}, u32[]{:S(2)}) copy-start(bf16[64,1024]{1,0:T(8,128)(2,1)} %param.17) | copy-start | bytes 393220
  15.1 16.0 %copy-start.2 = (bf16[64,1024]{1,0:T(8,128)(2,1)S(1)}, bf16[64,1024]{1,0:T(8,128)(2,1)}, u32[]{:S(2)}) copy-start(bf16[64,1024]{1,0:T(8,128)(2,1)} %param.18) | copy-start | bytes 393220
  21.9 9.6 %copy-start.10 = (f32[16,64]{1,0:T(8,128)S(1)}, f32[16,64]{1,0:T(8,128)}, u32[]{:S(2)}) copy-start(f32[16,64]{1,0:T(8,128)} %param.21) | copy-start | bytes 12292
  21.9 9.9 %copy-start.12 = (s32[1,64]{1,0:T(1,128)S(1)}, s32[1,64]{1,0:T(1,128)}, u32[]{:S(2)}) copy-start(s32[1,64]{1,0:T(1,128)} %param.23) | copy-start | bytes 772
  21.9 10.1 %copy-start.5 = (f32[16,64]{1,0:T(8,128)S(1)}, f32[16,64]{1,0:T(8,128)}, u32[]{:S(2)}) copy-start(f32[16,64]{1,0:T(8,128)} %param.22) | copy-start | bytes 12292
  21.9 90.3 %copy-start.4 = (s32[64,16]{0,1:T(8,128)S(1)}, s32[64,16]{0,1:T(8,128)}, u32[]{:S(2)}) copy-start(s32[64,16]{0,1:T(8,128)} %param.27) | copy-start | bytes 12292
  22.6 106.0 %all-to-all-start = ((bf16[32,1,32]{2,1,0:T(2,128)(2,1)}), bf16[32,1,32]{2,1,0:T(2,128)(2,1)S(1)}, u32[]{:S(2)}, u32[]{:S(2)}) async-start(bf16[32,1,32]{2,1,0:T(2,128)(2,1)} %convert_element_type.119), calls=%async_computation | async-start | bytes 32768 | tf_op jit(solution)/shard_map/all_to_all | solution.py:159
  116.3 7.0 %copy-start.11 = (f32[128]{0:T(128)S(1)}, f32[128]{0:T(128)}, u32[]{:S(2)}) copy-start(f32[128]{0:T(128)} %param.24) | copy-start | bytes 1540
  123.4 11.2 %copy-start.8 = (f32[2048]{0:T(1024)S(1)}, f32[2048]{0:T(1024)}, u32[]{:S(2)}) copy-start(f32[2048]{0:T(1024)} %param.26) | copy-start | bytes 24580
  128.6 13.2 %all-to-all-start.2 = ((s32[32,1,512]{2,1,0:T(1,128)}), s32[32,1,512]{2,1,0:T(1,128)S(1)}, u32[]{:S(2)}, u32[]{:S(2)}) async-start(s32[32,1,512]{2,1,0:T(1,128)} %reshape.395), calls=%async_computation.2 | async-start | bytes 131072 | tf_op jit(solution)/shard_map/all_to_all | solution.py:157
  141.8 99.0 %all-to-all-start.1 = ((bf16[32,32,2048]{2,1,0:T(8,128)(2,1)}), bf16[32,32,2048]{2,1,0:T(8,128)(2,1)}, u32[]{:S(2)}, u32[]{:S(2)}) async-start(bf16[32,32,2048]{2,1,0:T(8,128)(2,1)} %bitcast.128), calls=%async_computation.1 | async-start | bytes 8388608 | tf_op jit(solution)/shard_map/all_to_all | solution.py:156
  240.8 6.2 %copy-start.13 = (bf16[1,2048,1024]{2,1,0:T(8,128)(2,1)S(1)}, bf16[1,2048,1024]{2,1,0:T(8,128)(2,1)}, u32[]{:S(2)}) copy-start(bf16[1,2048,1024]{2,1,0:T(8,128)(2,1)} %param.30) | copy-start | bytes 12582916
  256.0 4.3 %copy-start.7 = (s32[640]{0:T(1024)S(1)}, s32[640]{0:T(1024)}, u32[]{:S(2)}) copy-start(s32[640]{0:T(1024)} %copy-done.6) | copy-start | bytes 7684
  256.0 98.2 %all-to-all-start.3 = ((bf16[32,32,2048]{2,1,0:T(8,128)(2,1)}), bf16[32,32,2048]{2,1,0:T(8,128)(2,1)}, u32[]{:S(2)}, u32[]{:S(2)}) async-start(bf16[32,32,2048]{2,1,0:T(8,128)(2,1)} %bitcast.134), calls=%async_computation.3 | async-start | bytes 8388608 | tf_op jit(solution)/shard_map/all_to_all | solution.py:169
Sparse Core Ops, SparseCore 0:
  8.9 22.5 all-gather.1
where the time goes:
time: 383 us
  waiting for transfers between devices  174 us (45%)
  other arithmetic  95.3 us (25%)
  local copies, waits for them, and re-layouts  56.1 us (15%)
  starting transfers between devices  22.5 us (6%)
  matrix products  21 us (5%)
  between operations  14 us (4%)
    all_to_all x1, waiting for transfers between devices, per_device(): lax.all_to_all(answer, ('ep', 'sub'), split_axis=0, concat_axis=0, tiled=...  93.8 us
    another operation x1, other arithmetic, delta_rule(): lax.linalg.triangular_solve(identity + mixing, target, left_side=True, lo...  79.3 us
    all_to_all x1, waiting for transfers between devices, per_device(): lax.all_to_all(send_quant, ('ep', 'sub'), split_axis=0, concat_axis=0, ti...  78.2 us
    mul x2, local copies, waits for them, and re-layouts, restore(): scaled = scaled * jnp.exp2(exponents.astype(jnp.float32))[..., None]  13.9 us
    gather x1, local copies, waits for them, and re-layouts, per_device(): gathered = returned.reshape(devices * capacity, model_width)[slot_index]  9.68 us
  transfers between devices with their start and end apart: 5, of which 3 were waited for; matrix products, arithmetic and copies ran while one was open for 35% of the time, Pallas kernels for 0%

commit v1 on v0

v1 whole, which is shorter than its diff:
```python
import functools

import jax
import jax.numpy as jnp
from jax import lax
from jax.experimental import pallas as pl
from jax.experimental.pallas import tpu as pltpu
from jax.sharding import PartitionSpec as P

KEY_HEADS = 8
HEAD = 128
QBLOCK = 128
LANES = 128
F32 = jnp.float32
BF16 = jnp.bfloat16
HIGHEST = lax.Precision.HIGHEST


def dot(a, b, precision=None):
    return jnp.dot(a, b, preferred_element_type=F32, precision=precision)


def dot_nt(a, b, precision=None):
    return lax.dot_general(
        a, b, (((1,), (1,)), ((), ())), preferred_element_type=F32, precision=precision
    )


def halves(a):
    high = a.astype(BF16)
    return high, (a - high.astype(F32)).astype(BF16)


def dot3(a, b):
    return dot(a[0], b[0]) + dot(a[0], b[1]) + dot(a[1], b[0])


def silu(v):
    return v / (1.0 + jnp.exp(-v))


def mixer(q_ref, k_ref, v_ref, gate_ref, decay_ref, rate_ref, seg_ref, gain_ref, gated):
    tokens = q_ref.shape[0]
    wide = 2 * tokens
    row = lax.broadcasted_iota(jnp.int32, (tokens, wide), 0)
    lane = lax.broadcasted_iota(jnp.int32, (tokens, wide), 1)
    first = lane < tokens
    col = jnp.where(first, lane, lane - tokens)
    diagonal = row == col
    eye2 = jnp.where(diagonal, 1.0, 0.0)
    upper2 = jnp.where(row <= col, 1.0, 0.0)
    r1 = lax.broadcasted_iota(jnp.int32, (tokens, tokens), 0)
    c1 = lax.broadcasted_iota(jnp.int32, (tokens, tokens), 1)
    eye1 = jnp.where(r1 == c1, 1.0, 0.0)
    lower1 = jnp.where(r1 >= c1, 1.0, 0.0)
    decay = decay_ref[...]
    cum_rows = dot(decay, upper2, HIGHEST)
    cum_cols = dot_nt(lower1, decay, HIGHEST)
    rates = dot(rate_ref[...], eye2, HIGHEST)
    segments = seg_ref[...].astype(F32)
    seg_row = dot(jnp.broadcast_to(segments, (8, tokens)), eye2, HIGHEST)[:1]
    seg_col = dot_nt(eye1, jnp.broadcast_to(segments, (8, tokens)), HIGHEST)[:, :1]
    kept = (row >= col) & (jnp.abs(seg_row - seg_col) < 0.5)
    strict = row > col
    bi = lax.broadcasted_iota(jnp.int32, (wide, wide), 0)
    bj = lax.broadcasted_iota(jnp.int32, (wide, wide), 1)
    identity = jnp.where(bi == bj, 1.0, 0.0)
    first_row = first[:1]
    gain = gain_ref[...]

    def stack(pair_matrix):
        return jnp.concatenate(
            [jnp.where(first, pair_matrix, 0.0), jnp.where(first, 0.0, pair_matrix)], axis=0
        )

    for p in range(KEY_HEADS):
        a, b = 2 * p, 2 * p + 1
        q = q_ref[:, p * HEAD : (p + 1) * HEAD]
        k = k_ref[:, p * HEAD : (p + 1) * HEAD]
        twice = jnp.concatenate([k, k], axis=0)
        kk = dot_nt(k, twice)
        qk = dot_nt(q, twice)
        own = jnp.where(diagonal, kk, 0.0)
        key_col = lax.rsqrt(jnp.sum(own, axis=1, keepdims=True) * 0.5 + 1e-06)
        key_row = lax.rsqrt(jnp.sum(own, axis=0, keepdims=True) + 1e-06)
        q_wide = q.astype(F32)
        query_col = lax.rsqrt(jnp.sum(q_wide * q_wide, axis=1, keepdims=True) + 1e-06)
        cum_col = jnp.where(first, cum_cols[:, a : a + 1], cum_cols[:, b : b + 1])
        cum_row = jnp.where(first_row, cum_rows[a : a + 1], cum_rows[b : b + 1])
        rate = jnp.where(first_row, rates[a : a + 1], rates[b : b + 1])
        decayed = jnp.where(kept, jnp.exp(jnp.where(kept, cum_col - cum_row, 0.0)), 0.0)
        weighted = decayed * (rate * key_row)
        mixing = stack(jnp.where(strict, weighted * (kk * key_col), 0.0))
        scores = stack(weighted * (qk * query_col))

        def between(level):
            return jnp.where(
                ((bi >> level) == (bj >> level)) & ((bi >> (level - 1)) != (bj >> (level - 1))),
                mixing,
                0.0,
            )

        inverse = identity - between(1)
        level = 2
        while (1 << level) <= tokens:
            split = halves(inverse)
            inner = dot3(halves(between(level)), split)
            inverse = inverse - dot3(split, halves(inner))
            level += 1
        values = jnp.concatenate(
            [v_ref[:, a * HEAD : (a + 1) * HEAD], v_ref[:, b * HEAD : (b + 1) * HEAD]], axis=0
        )
        split = halves(inverse)
        update = dot(split[0], values) + dot(split[1], values)
        mixed = dot3(halves(scores), halves(update))
        mixed = mixed * lax.rsqrt(jnp.mean(mixed * mixed, axis=1, keepdims=True) + 1e-06) * gain
        for at, head in ((0, a), (1, b)):
            gate = gate_ref[:, head * HEAD : (head + 1) * HEAD].astype(F32)
            gated[:, head * HEAD : (head + 1) * HEAD] = (
                mixed[at * tokens : (at + 1) * tokens] * silu(gate)
            ).astype(BF16)


def kernel(
    depth,
    resid_ref, q_ref, k_ref, v_ref, gate_ref, decay_ref, rate_ref, seg_ref, gain_ref,
    post_ref, exps_ref, ids_ref, weights_ref, proj_hbm, gate_up_hbm, down_hbm,
    out_ref,
    gated, proj, gate_up, down, hidden, wide_hidden, rows, terms, inner, from_b, from_a, from_z,
    load_sem, pair_send, pair_recv, ag_send, ag_recv, b_send, b_recv, a_send, a_recv, z_send, z_recv,
):
    tokens, width = resid_ref.shape
    part_rows = tokens // 2
    half = down.shape[1]
    ep = lax.axis_index("ep")
    core = lax.axis_index("sub")
    z, y, x = ep // 4, (ep // 2) % 2, ep % 2

    def at(zz, yy, xx):
        return {"ep": zz * 4 + yy * 2 + xx}

    def z_away(d):
        return lax.rem(z + d, depth)

    x_next, y_next = at(z, y, 1 - x), at(z, 1 - y, x)
    sibling = {"sub": 1 - core}
    peers = [at(z_away(d), y, x) for d in range(1, depth)] + [x_next, y_next, sibling]
    barrier = pltpu.get_barrier_semaphore()
    for peer in peers:
        pl.semaphore_signal(
            barrier, inc=1, device_id=peer, device_id_type=pl.DeviceIdType.MESH
        )
    pl.semaphore_wait(barrier, len(peers))

    def push(src, dst, send, recv, device):
        copy = pltpu.make_async_remote_copy(
            src_ref=src, dst_ref=dst, send_sem=send, recv_sem=recv,
            device_id=device, device_id_type=pl.DeviceIdType.MESH,
        )
        copy.start()
        return copy

    shared = [(proj_hbm, proj), (gate_up_hbm, gate_up), (down_hbm, down)]
    loads, swaps = [], []
    for i, (src, dst) in enumerate(shared):
        mine = dst.at[core] if i == 0 else dst.at[0]
        there = dst.at[core] if i == 0 else dst.at[1]
        swaps.append(push(src, there, pair_send.at[i], pair_recv.at[i], sibling))
        load = pltpu.make_async_copy(src, mine, load_sem.at[i])
        load.start()
        loads.append(load)

    mixer(q_ref, k_ref, v_ref, gate_ref, decay_ref, rate_ref, seg_ref, gain_ref, gated)

    loads[0].wait()
    swaps[0].wait_recv()
    tile = 512

    @pl.loop(0, width // tile)
    def _(j):
        cols = pl.ds(pl.multiple_of(j * tile, tile), tile)
        depth_half = proj.shape[1]
        total = dot(gated[:, :depth_half], proj[0, :, cols])
        total = total + dot(gated[:, depth_half:], proj[1, :, cols])
        hidden[:, cols] = (resid_ref[:, cols].astype(F32) + total).astype(BF16)

    wide_hidden[...] = hidden[...].astype(F32)
    scale = lax.rsqrt(
        jnp.mean(wide_hidden[...] * wide_hidden[...], axis=1, keepdims=True) + 1e-06
    )
    for j in range(width // QBLOCK):
        cols = slice(j * QBLOCK, (j + 1) * QBLOCK)
        exps = exps_ref[:, j : j + 1]
        power = jnp.zeros(exps.shape, F32)
        unpower = jnp.zeros(exps.shape, F32)
        for e in range(-9, -4):
            power = jnp.where(exps == e, 2.0**e, power)
            unpower = jnp.where(exps == e, 2.0**-e, unpower)
        block = wide_hidden[:, cols] * scale * post_ref[:, cols] * unpower
        block = jnp.clip(block, -448.0, 448.0).astype(BF16).astype(F32)
        block = (block * power).astype(BF16)
        for p in range(2):
            rows[y, x, z, p, :, cols] = block[p * part_rows : (p + 1) * part_rows]
    lane = lax.broadcasted_iota(jnp.int32, (tokens, LANES), 1)
    name = jnp.where(lane < LANES // 2, lane, lane - LANES // 2)
    dense = jnp.zeros((tokens, LANES), F32)
    for choice in range(ids_ref.shape[1]):
        dense = dense + jnp.where(
            name == ids_ref[:, choice : choice + 1], weights_ref[:, choice : choice + 1], 0.0
        )
    high = dense.astype(BF16).astype(F32)
    dense = jnp.where(lane < LANES // 2, high, dense - high).astype(BF16)
    for p in range(2):
        rows[y, x, z, p, :, width:] = dense[p * part_rows : (p + 1) * part_rows]

    a_next, b_next = (y_next, x_next), (x_next, y_next)
    a_col, b_col = ((1 - y, x), (y, 1 - x)), ((y, 1 - x), (1 - y, x))
    far = (1 - y, 1 - x)
    sent = []

    def gather_send(p, slot, yy, xx, zz, device):
        block = rows.at[yy, xx, zz, p]
        sent.append(
            push(block, block, ag_send.at[p, slot], ag_recv.at[p, yy * 2 + xx, zz], device)
        )

    def gather_wait(p, yy, xx, zz):
        block = rows.at[yy, xx, zz, p]
        pltpu.make_async_remote_copy(
            src_ref=block, dst_ref=block, send_sem=ag_send.at[p, 0],
            recv_sem=ag_recv.at[p, yy * 2 + xx, zz],
            device_id=x_next, device_id_type=pl.DeviceIdType.MESH,
        ).wait_recv()

    order = sorted(range(1, depth), key=lambda d: min(d, depth - d))
    for d in order:
        for p in range(2):
            gather_send(p, d - 1, y, x, z, at(z_away(d), y, x))
    base_a, base_b = depth - 1, 2 * depth - 1
    for d in [0] + order:
        for p in range(2):
            zz = z_away(d)
            if d:
                gather_wait(p, y, x, zz)
            gather_send(p, base_a + d, y, x, zz, a_next[p])
            gather_send(p, base_b + d, y, x, zz, b_next[p])

    own_expert = ep * 2 + core
    other_expert = ep * 2 + 1 - core

    def ffn(yy, xx):
        count = depth * tokens
        batch = rows[yy, xx].reshape(count, width + LANES)
        lanes = lax.broadcasted_iota(jnp.int32, (count, LANES), 1)
        shares = batch[:, width:].astype(F32)
        weight = [
            jnp.sum(
                jnp.where((lanes == e) | (lanes == e + LANES // 2), shares, 0.0),
                axis=1, keepdims=True,
            )
            for e in (own_expert, other_expert)
        ]

        @pl.loop(0, 2)
        def _(e):
            batch_in = rows[yy, xx, :, :, :, :width].reshape(count, width)
            for cut in range(half // 256):
                gate = dot(batch_in, gate_up[e, :, cut * 256 : (cut + 1) * 256])
                up = dot(batch_in, gate_up[e, :, half + cut * 256 : half + (cut + 1) * 256])
                inner[e, :, cut * 256 : (cut + 1) * 256] = (silu(gate) * up).astype(BF16)

        @pl.loop(0, width // tile)
        def _(j):
            cols = pl.ds(pl.multiple_of(j * tile, tile), tile)
            total = weight[0] * dot(inner[0], down[0, :, cols])
            total = total + weight[1] * dot(inner[1], down[1, :, cols])
            terms[yy, xx, :, :, :, cols] = total.astype(BF16).reshape(
                depth, 2, part_rows, tile
            )

    for i in (1, 2):
        loads[i].wait()
        swaps[i].wait_recv()
    ffn(y, x)

    for d in [0] + order:
        for p in range(2):
            zz = z_away(d)
            yy, xx = a_col[p]
            gather_wait(p, yy, xx, zz)
            gather_send(p, base_b + depth + d, yy, xx, zz, b_next[p])

    def b_stage(p, rel, yy, xx):
        for d in order + [0]:
            zz = z_away(d)
            sent.append(
                push(
                    terms.at[yy, xx, zz, p], from_b.at[p, rel, zz],
                    b_send.at[p, rel, zz], b_recv.at[p, rel, zz], b_next[p],
                )
            )

    for p in (0, 1):
        for d in [0] + order:
            yy, xx = b_col[p]
            gather_wait(p, yy, xx, z_away(d))
        if p == 0:
            ffn(*b_col[0])
            b_stage(0, 0, *b_col[0])
    ffn(*b_col[1])
    b_stage(1, 0, *b_col[1])
    for p in (0, 1):
        for d in [0] + order:
            gather_wait(p, far[0], far[1], z_away(d))
    ffn(*far)
    for p in (0, 1):
        b_stage(p, 1, *far)

    def arrived(buffer, recv):
        pltpu.make_async_remote_copy(
            src_ref=buffer, dst_ref=buffer, send_sem=b_send.at[0, 0, 0], recv_sem=recv,
            device_id=x_next, device_id_type=pl.DeviceIdType.MESH,
        ).wait_recv()

    for d in order + [0]:
        zz = z_away(d)
        for p in (0, 1):
            yy, xx = a_col[p]
            arrived(from_b.at[p, 1, zz], b_recv.at[p, 1, zz])
            total = terms[yy, xx, zz, p].astype(F32) + from_b[p, 1, zz].astype(F32)
            terms[yy, xx, zz, p] = total.astype(BF16)
            sent.append(
                push(
                    terms.at[yy, xx, zz, p], from_a.at[p, zz],
                    a_send.at[p, zz], a_recv.at[p, zz], a_next[p],
                )
            )
    for d in order + [0]:
        zz = z_away(d)
        for p in (0, 1):
            arrived(from_b.at[p, 0, zz], b_recv.at[p, 0, zz])
            arrived(from_a.at[p, zz], a_recv.at[p, zz])
            total = (
                terms[y, x, zz, p].astype(F32)
                + from_b[p, 0, zz].astype(F32)
                + from_a[p, zz].astype(F32)
            )
            if d:
                terms[y, x, zz, p] = total.astype(BF16)
                sent.append(
                    push(
                        terms.at[y, x, zz, p], from_z.at[p, d],
                        z_send.at[p, d], z_recv.at[p, d], at(zz, y, x),
                    )
                )
            else:
                wide_hidden[p * part_rows : (p + 1) * part_rows] = (
                    wide_hidden[p * part_rows : (p + 1) * part_rows] + total
                )
    for p in (0, 1):
        total = wide_hidden[p * part_rows : (p + 1) * part_rows]
        for d in order:
            arrived(from_z.at[p, d], z_recv.at[p, d])
            total = total + from_z[p, d].astype(F32)
        out_ref[p * part_rows : (p + 1) * part_rows] = total.astype(BF16)
    for copy in swaps + sent:
        copy.wait_send()


def per_device(
    resid_in, query_input, key_input, value_input, gate_input, decay_log, write_rate, segments,
    head_gain, out_proj, post_gain, block_exps, route_ids, route_weights, w_gate_up, w_down,
):
    tokens, width = resid_in.shape
    depth = lax.axis_size("ep") // 4
    part = tokens // 2
    hidden_units = w_down.shape[1]
    vmem = pl.BlockSpec(memory_space=pltpu.VMEM)
    hbm = pl.BlockSpec(memory_space=pl.ANY)
    dma = pltpu.SemaphoreType.DMA
    return pl.pallas_call(
        functools.partial(kernel, depth),
        out_shape=jax.ShapeDtypeStruct((tokens, width), BF16),
        in_specs=[vmem] * 13 + [hbm] * 3,
        out_specs=vmem,
        scratch_shapes=[
            pltpu.VMEM((tokens, width), BF16),
            pltpu.VMEM((2,) + out_proj.shape, BF16),
            pltpu.VMEM((2,) + w_gate_up.shape[1:], BF16),
            pltpu.VMEM((2,) + w_down.shape[1:], BF16),
            pltpu.VMEM((tokens, width), BF16),
            pltpu.VMEM((tokens, width), F32),
            pltpu.VMEM((2, 2, depth, 2, part, width + LANES), BF16),
            pltpu.VMEM((2, 2, depth, 2, part, width), BF16),
            pltpu.VMEM((2, depth * tokens, hidden_units), BF16),
            pltpu.VMEM((2, 2, depth, part, width), BF16),
            pltpu.VMEM((2, depth, part, width), BF16),
            pltpu.VMEM((2, depth, part, width), BF16),
            dma((3,)), dma((3,)), dma((3,)),
            dma((2, 4 * depth - 1)), dma((2, 4, depth)),
            dma((2, 2, depth)), dma((2, 2, depth)),
            dma((2, depth)), dma((2, depth)),
            dma((2, depth)), dma((2, depth)),
        ],
        compiler_params=pltpu.CompilerParams(
            collective_id=0, has_side_effects=True, vmem_limit_bytes=60 * 1024 * 1024
        ),
        cost_estimate=pl.CostEstimate(
            flops=14_000_000_000, bytes_accessed=24_000_000, transcendentals=2_000_000
        ),
    )(
        resid_in, query_input, key_input, value_input, gate_input, decay_log, write_rate, segments,
        head_gain.reshape(1, -1), post_gain.reshape(1, -1), block_exps, route_ids, route_weights,
        out_proj, w_gate_up[0], w_down[0],
    )


def solution(mesh):
    rows = P(("grp", "ep", "sub"), None)
    return jax.shard_map(
        per_device,
        mesh=mesh,
        in_specs=(
            rows, rows, rows, rows, rows,
            P(None, ("grp", "ep", "sub")),
            P(None, ("grp", "ep", "sub")),
            rows,
            P(),
            P("sub", None),
            P(),
            rows, rows, rows,
            P(("ep", "sub"), None, None),
            P(("ep", "sub"), None, None),
        ),
        out_specs=rows,
        check_vma=False,
    )
```

time: 383 us -> 128 us (0.33)
  waiting for transfers between devices: 174 us -> 0 us
  Pallas kernels: 0 us -> 122 us
  other arithmetic: 95.3 us -> 0 us
  local copies, waits for them, and re-layouts: 56.1 us -> 5.83 us
  starting transfers between devices: 22.5 us -> 0 us
  matrix products: 21 us -> 0 us
  between operations: 14 us -> 0.01 us
    all_to_all x4 -> x0, waiting for transfers between devices: 173 us -> none  [the longest x1 93.8 us: per_device(): lax.all_to_all(answer, ('ep', 'sub'), split_axis=0, concat_axis=0, tiled=...]
    pallas_call x0 -> x1, Pallas kernels: none -> 122 us  [per_device(): pl.pallas_call(functools.partial(kernel, depth), out_shape=jax.ShapeDtype...]
    another operation x4 -> x0, other arithmetic: 81 us -> none  [the longest x1 79.3 us: delta_rule(): lax.linalg.triangular_solve(identity + mixing, target, left_side=True, lo...]
    gather x5 -> x0, local copies, waits for them, and re-layouts: 25.5 us -> none  [the longest x1 9.68 us: per_device(): gathered = returned.reshape(devices * capacity, model_width)[slot_index]]
    all_to_all x4 -> x0, starting transfers between devices: 22.5 us -> none  [the longest x1 7.3 us: per_device(): lax.all_to_all(send_weights.astype(jnp.bfloat16), ('ep', 'sub'), split_ax...]
    dot_general x8 -> x0, matrix products: 19 us -> none  [the longest x1 5.16 us: per_device(): jnp.dot(gated_out, lax.all_gather(out_proj, 'sub', axis=0, tiled=True), p...]
    mul x6 -> x0, local copies, waits for them, and re-layouts: 14.9 us -> none  [the longest x2 13.9 us: restore(): scaled = scaled * jnp.exp2(exponents.astype(jnp.float32))[..., None]]
    convert_element_type x6 -> x0, other arithmetic: 7.29 us -> none  [the longest x1 6.22 us: restore(): return scaled.astype(jnp.bfloat16).reshape(shape)]
  transfers between devices with their start and end apart: 5 -> 0, of which waited for: 3 -> 0; matrix products, arithmetic and copies ran while one was open for 35% -> 0% of each run, Pallas kernels for 0% -> 0%
where the time goes in v1:
time: 128 us; the launch traced here: 127 us
  Pallas kernels  122 us (95%)
  local copies, waits for them, and re-layouts  5.83 us (5%)
    pallas_call x1, Pallas kernels, per_device(): pl.pallas_call(functools.partial(kernel, depth), out_shape=jax.ShapeDtype...  122 us
    unnamed x4, local copies, waits for them, and re-layouts  5.83 us

profile of v1, /device:TPU:0, one launch (start us, length us, event | category | flops | bytes accessed | tf_op | source)
XLA Modules:
  0.0 127.4 jit_solution(9228794280146151566)
XLA Ops:
  0.0 1.4 %copy.17.exps_ref = s32[64,16]{1,0:T(8,128)} copy(s32[64,16]{0,1:T(8,128)} %param.27) | data formatting | bytes 8192 | tf_op args[11]
  1.4 1.4 %copy.18.ids_ref = s32[64,10]{1,0:T(8,128)} copy(s32[64,10]{0,1:T(8,128)} %param.28) | data formatting | bytes 5120 | tf_op args[12]
  2.8 1.4 %copy.19.weights_ref = f32[64,10]{1,0:T(8,128)} copy(f32[64,10]{0,1:T(8,128)} %param.29) | data formatting | bytes 5120 | tf_op args[13]
  4.2 121.6 %shard_map.154 = bf16[64,2048]{1,0:T(8,128)(2,1)} custom-call(bf16[64,2048]{1,0:T(8,128)(2,1)} %resid_ref.1, bf16[64,1024]{1,0:T(8,128)(2,1)} %q_ref.1, bf16[64,1024]{1,0:T(8,128)(2,1)} %k_ref.1, bf16[64,2048]{1,0:T(8,128)(2,1)} %v_ref.1, bf16[64,2048]{1,0:T(8,128)(2,1)} %gate_ref.1, f32[16,64]{1,0:T(8,128)} %decay_ref.1, f32[16,64]{1,0:T(8,128)} %rate_ref.1, ...), custom_call_target="tpu_custom_call" | custom-call | flops 14000000000 | bytes 24000000 | tf_op jit(solution)/shard_map/pallas_call | solution.py:381
  125.7 1.7 %copy.21 = bf16[64,2048]{1,0:T(8,128)(2,1)} copy(bf16[64,2048]{1,0:T(8,128)(2,1)} %shard_map.154) | data formatting | bytes 524288

commit v2 on v1

--- a/solution.py
+++ b/solution.py
@@ -188,9 +188,15 @@
     scale = lax.rsqrt(
         jnp.mean(wide_hidden[...] * wide_hidden[...], axis=1, keepdims=True) + 1e-06
     )
+    r1 = lax.broadcasted_iota(jnp.int32, (tokens, tokens), 0)
+    c1 = lax.broadcasted_iota(jnp.int32, (tokens, tokens), 1)
+    eye = jnp.where(r1 == c1, 1.0, 0.0)
+    all_exps = dot_nt(eye, exps_ref[...].astype(F32), HIGHEST)
+    ids = dot_nt(eye, ids_ref[...].astype(F32), HIGHEST)
+    weights = dot_nt(eye, weights_ref[...], HIGHEST)
     for j in range(width // QBLOCK):
         cols = slice(j * QBLOCK, (j + 1) * QBLOCK)
-        exps = exps_ref[:, j : j + 1]
+        exps = all_exps[:, j : j + 1]
         power = jnp.zeros(exps.shape, F32)
         unpower = jnp.zeros(exps.shape, F32)
         for e in range(-9, -4):
@@ -202,11 +208,11 @@
         for p in range(2):
             rows[y, x, z, p, :, cols] = block[p * part_rows : (p + 1) * part_rows]
     lane = lax.broadcasted_iota(jnp.int32, (tokens, LANES), 1)
-    name = jnp.where(lane < LANES // 2, lane, lane - LANES // 2)
+    name = jnp.where(lane < LANES // 2, lane, lane - LANES // 2).astype(F32)
     dense = jnp.zeros((tokens, LANES), F32)
-    for choice in range(ids_ref.shape[1]):
+    for choice in range(ids_ref.shape[0]):
         dense = dense + jnp.where(
-            name == ids_ref[:, choice : choice + 1], weights_ref[:, choice : choice + 1], 0.0
+            name == ids[:, choice : choice + 1], weights[:, choice : choice + 1], 0.0
         )
     high = dense.astype(BF16).astype(F32)
     dense = jnp.where(lane < LANES // 2, high, dense - high).astype(BF16)
@@ -237,13 +243,29 @@
         for p in range(2):
             gather_send(p, d - 1, y, x, z, at(z_away(d), y, x))
     base_a, base_b = depth - 1, 2 * depth - 1
-    for d in [0] + order:
+
+    def along_z(d):
         for p in range(2):
             zz = z_away(d)
             if d:
                 gather_wait(p, y, x, zz)
             gather_send(p, base_a + d, y, x, zz, a_next[p])
             gather_send(p, base_b + d, y, x, zz, b_next[p])
+
+    def along_a(d):
+        for p in range(2):
+            zz = z_away(d)
+            yy, xx = a_col[p]
+            gather_wait(p, yy, xx, zz)
+            gather_send(p, base_b + depth + d, yy, xx, zz, b_next[p])
+
+    along_z(0)
+    along_a(0)
+    for i, d in enumerate(order):
+        along_z(d)
+        if i:
+            along_a(order[i - 1])
+    along_a(order[-1])
 
     own_expert = ep * 2 + core
     other_expert = ep * 2 + 1 - core
@@ -283,15 +305,10 @@
         swaps[i].wait_recv()
     ffn(y, x)
 
-    for d in [0] + order:
-        for p in range(2):
-            zz = z_away(d)
-            yy, xx = a_col[p]
-            gather_wait(p, yy, xx, zz)
-            gather_send(p, base_b + depth + d, yy, xx, zz, b_next[p])
+    back = order[::-1] + [0]
 
     def b_stage(p, rel, yy, xx):
-        for d in order + [0]:
+        for d in back:
             zz = z_away(d)
             sent.append(
                 push(
@@ -322,7 +339,7 @@
             device_id=x_next, device_id_type=pl.DeviceIdType.MESH,
         ).wait_recv()
 
-    for d in order + [0]:
+    def reduce_a(d):
         zz = z_away(d)
         for p in (0, 1):
             yy, xx = a_col[p]
@@ -335,7 +352,8 @@
                     a_send.at[p, zz], a_recv.at[p, zz], a_next[p],
                 )
             )
-    for d in order + [0]:
+
+    def reduce_z(d):
         zz = z_away(d)
         for p in (0, 1):
             arrived(from_b.at[p, 0, zz], b_recv.at[p, 0, zz])
@@ -357,6 +375,12 @@
                 wide_hidden[p * part_rows : (p + 1) * part_rows] = (
                     wide_hidden[p * part_rows : (p + 1) * part_rows] + total
                 )
+
+    for i, d in enumerate(back):
+        reduce_a(d)
+        if i:
+            reduce_z(back[i - 1])
+    reduce_z(back[-1])
     for p in (0, 1):
         total = wide_hidden[p * part_rows : (p + 1) * part_rows]
         for d in order:
@@ -410,7 +434,7 @@
         ),
     )(
         resid_in, query_input, key_input, value_input, gate_input, decay_log, write_rate, segments,
-        head_gain.reshape(1, -1), post_gain.reshape(1, -1), block_exps, route_ids, route_weights,
+        head_gain.reshape(1, -1), post_gain.reshape(1, -1), block_exps.T, route_ids.T, route_weights.T,
         out_proj, w_gate_up[0], w_down[0],
     )
 

time: 128 us -> 121 us (0.945)
  local copies, waits for them, and re-layouts: 5.83 us -> 1.67 us
  Pallas kernels: 122 us -> 119 us
    unnamed x4 -> x1, local copies, waits for them, and re-layouts: 5.83 us -> 1.67 us
    pallas_call x1, Pallas kernels: 122 us -> 119 us  [per_device(): pl.pallas_call(functools.partial(kernel, depth), out_shape=jax.ShapeDtype...]
where the time goes in v2:
time: 121 us
  Pallas kernels  119 us (98%)
  local copies, waits for them, and re-layouts  1.67 us (1%)
    pallas_call x1, Pallas kernels, per_device(): pl.pallas_call(functools.partial(kernel, depth), out_shape=jax.ShapeDtype...  119 us

profile of v2, /device:TPU:0, one launch (start us, length us, event | category | flops | bytes accessed | tf_op | source)
XLA Modules:
  0.0 120.5 jit_solution(6118676797570932123)
XLA Ops:
  0.0 118.8 %shard_map.154 = bf16[64,2048]{1,0:T(8,128)(2,1)} custom-call(bf16[64,2048]{1,0:T(8,128)(2,1)} %resid_ref.1, bf16[64,1024]{1,0:T(8,128)(2,1)} %q_ref.1, bf16[64,1024]{1,0:T(8,128)(2,1)} %k_ref.1, bf16[64,2048]{1,0:T(8,128)(2,1)} %v_ref.1, bf16[64,2048]{1,0:T(8,128)(2,1)} %gate_ref.1, f32[16,64]{1,0:T(8,128)} %decay_ref.1, f32[16,64]{1,0:T(8,128)} %rate_ref.1, ...), custom_call_target="tpu_custom_call" | custom-call | flops 14000000000 | bytes 24000000 | tf_op jit(solution)/shard_map/pallas_call | solution.py:405
  118.9 1.7 %copy.18 = bf16[64,2048]{1,0:T(8,128)(2,1)} copy(bf16[64,2048]{1,0:T(8,128)(2,1)} %shard_map.154) | data formatting | bytes 524288

commit v3 on v2

--- a/solution.py
+++ b/solution.py
@@ -307,8 +307,8 @@
 
     back = order[::-1] + [0]
 
-    def b_stage(p, rel, yy, xx):
-        for d in back:
+    def b_stage(p, rel, yy, xx, which):
+        for d in which:
             zz = z_away(d)
             sent.append(
                 push(
@@ -323,15 +323,16 @@
             gather_wait(p, yy, xx, z_away(d))
         if p == 0:
             ffn(*b_col[0])
-            b_stage(0, 0, *b_col[0])
+            b_stage(0, 0, *b_col[0], back[:2])
     ffn(*b_col[1])
-    b_stage(1, 0, *b_col[1])
+    b_stage(1, 0, *b_col[1], back[:2])
     for p in (0, 1):
         for d in [0] + order:
             gather_wait(p, far[0], far[1], z_away(d))
     ffn(*far)
-    for p in (0, 1):
-        b_stage(p, 1, *far)
+    for d in back[:2]:
+        for p in (0, 1):
+            b_stage(p, 1, *far, [d])
 
     def arrived(buffer, recv):
         pltpu.make_async_remote_copy(
@@ -378,6 +379,10 @@
 
     for i, d in enumerate(back):
         reduce_a(d)
+        for p in (0, 1):
+            if i:
+                b_stage(p, 0, *b_col[p], back[i + 1 : i + 2])
+            b_stage(p, 1, *far, back[i + 2 : i + 3])
         if i:
             reduce_z(back[i - 1])
     reduce_z(back[-1])

time: 121 us -> 116 us (0.959)
  Pallas kernels: 119 us -> 115 us
    pallas_call x1, Pallas kernels: 119 us -> 115 us  [per_device(): pl.pallas_call(functools.partial(kernel, depth), out_shape=jax.ShapeDtype...]
where the time goes in v3:
time: 116 us
  Pallas kernels  115 us (99%)
  local copies, waits for them, and re-layouts  1.67 us (1%)
    pallas_call x1, Pallas kernels, per_device(): pl.pallas_call(functools.partial(kernel, depth), out_shape=jax.ShapeDtype...  115 us

profile of v3, /device:TPU:0, one launch (start us, length us, event | category | flops | bytes accessed | tf_op | source)
XLA Modules:
  0.0 116.3 jit_solution(15304458164903170576)
XLA Ops:
  0.0 114.6 %shard_map.154 = bf16[64,2048]{1,0:T(8,128)(2,1)} custom-call(bf16[64,2048]{1,0:T(8,128)(2,1)} %resid_ref.1, bf16[64,1024]{1,0:T(8,128)(2,1)} %q_ref.1, bf16[64,1024]{1,0:T(8,128)(2,1)} %k_ref.1, bf16[64,2048]{1,0:T(8,128)(2,1)} %v_ref.1, bf16[64,2048]{1,0:T(8,128)(2,1)} %gate_ref.1, f32[16,64]{1,0:T(8,128)} %decay_ref.1, f32[16,64]{1,0:T(8,128)} %rate_ref.1, ...), custom_call_target="tpu_custom_call" | custom-call | flops 14000000000 | bytes 24000000 | tf_op jit(solution)/shard_map/pallas_call | solution.py:410
  114.7 1.7 %copy.18 = bf16[64,2048]{1,0:T(8,128)(2,1)} copy(bf16[64,2048]{1,0:T(8,128)(2,1)} %shard_map.154) | data formatting | bytes 524288
